TPU v7x, 256 devices: a whole 4x4x8 slice. The times are simulated.
256 devices in a mesh: visit: 32 (over y, z), tile: 8 (over x, core).
Axes of the slice: x: 4, y: 4, z: 8, core: 2. Of those that a mesh axis runs over, the one named last changes fastest.
Arguments:
- science: float32 [32, 512, 4096], P('visit', 'tile'), may hold values from -8 to 8
- science_var: float32 [32, 512, 4096], P('visit', 'tile'), may hold values from 0.5 to 4
- template: float32 [32, 512, 4096], P('visit', 'tile'), may hold values from -8 to 8
- template_var: float32 [32, 512, 4096], P('visit', 'tile'), may hold values from 0.1 to 1
- intersection: int32 [32, 32, 1], replicated, may hold values from 0 to 31; in each aligned block of 32 rows (0 to 31, 32 to 63, ..., all dimensions but the last counted through in order) at most 2 rows name the same one
- col_offset: int32 [32, 32], replicated, may hold values from 0 to 3968
- basis_row: float32 [16, 41], replicated, may hold values from -1 to 1
- basis_col: float32 [16, 41], replicated, may hold values from -1 to 1
- coef_sets: float32 [8, 16], replicated, may hold values from -1.5 to 1.5
- tile_coef: int32 [32, 8], replicated, may hold values from 0 to 7
Outputs:
- difference: float32 [32, 512, 4096], P('visit', 'tile')
- difference_var: float32 [32, 512, 4096], P('visit', 'tile')
Inputs may be any that keep to these rules, and one draw needn't show every extreme that they name: `intersection`: no visit takes more than 2 of its 32 pieces from one owner, and some visit takes exactly 2 from one owner.
All inputs are finite; a program needn't handle non-finite values.
Results may differ from a plain program's by a relative error of at most 0.0003.
Values sent between devices are 32-bit elements; how exact they have to be, the bound alone decides.
A program may use at most 320 MiB of HBM per device.

v0:
```python
import jax
import jax.numpy as jnp
from jax import lax
from jax.sharding import PartitionSpec as P

PIECE = 128
KP = 32
KW = 41
NB = 16
NSETS = 8


def with_halo(cells, sides, width):
    for axis, dim in sides:
        count = lax.axis_size(axis)
        ends = count - 1
        head = lax.slice_in_dim(cells, 0, width, axis=dim)
        tail = lax.slice_in_dim(cells, cells.shape[dim] - width, cells.shape[dim], axis=dim)
        cells = jnp.concatenate(
            [
                lax.ppermute(tail, axis, [(i, (i + 1) % count) for i in range(ends)]),
                cells,
                lax.ppermute(head, axis, [((i + 1) % count, i) for i in range(ends)]),
            ],
            axis=dim,
        )
    return cells


def column_windows(operand, margin):
    padded = jnp.pad(operand, [(0, 0)] * (operand.ndim - 1) + [(margin, margin)])
    return jnp.stack(
        [
            padded[..., column_block * PIECE : column_block * PIECE + PIECE + 2 * margin]
            for column_block in range(KP)
        ],
        axis=-2,
    )


def local(
    science,
    science_var,
    template,
    template_var,
    intersection,
    col_offset,
    basis_row,
    basis_col,
    coef_sets,
    tile_coef,
):
    margin = (KW - 1) // 2
    visits = lax.axis_size("visit")
    slots = max(2, KP // visits)
    tile_rows = science.shape[1]
    tile_width = science.shape[2]
    owner_me = lax.axis_index("visit")
    tile_me = lax.axis_index("tile")
    highest = lax.Precision.HIGHEST
    chosen_set = lax.dynamic_slice(tile_coef, (owner_me, tile_me), (1, 1))[0, 0]
    selector = (jnp.arange(NSETS, dtype=jnp.int32) == chosen_set).astype(jnp.float32)
    coeffs = jnp.dot(selector, coef_sets, precision=highest)
    kernel = jnp.einsum("b,ba,bc->ac", coeffs, basis_row, basis_col, precision=highest)
    kernel_power = jnp.sum(kernel * kernel)
    col_shift = jnp.arange(PIECE + 2 * margin)[:, None] - jnp.arange(PIECE)[None, :]
    col_taps = (col_shift[:, :, None] == jnp.arange(KW)[None, None, :]).astype(jnp.float32)
    col_band = jnp.einsum("wcq,bq->bwc", col_taps, basis_col, precision=highest)
    row_shift = jnp.arange(tile_rows + 2 * margin)[None, :] - jnp.arange(tile_rows)[:, None]
    row_taps = (row_shift[:, :, None] == jnp.arange(KW)[None, None, :]).astype(jnp.float32)
    row_band = jnp.einsum("iaq,bq->iba", row_taps, coeffs[:, None] * basis_row, precision=highest)
    owner_of = intersection[:, :, 0]
    matches = owner_of == owner_me
    slot_rank = jnp.cumsum(matches.astype(jnp.int32), axis=1) - 1
    slot_pick = matches[:, None, :] & (
        slot_rank[:, None, :] == jnp.arange(slots, dtype=jnp.int32)[None, :, None]
    )
    starts = jnp.sum(jnp.where(slot_pick, col_offset[:, None, :], 0), axis=2)
    filled = jnp.any(slot_pick, axis=2).astype(jnp.float32)
    owned_patch = jnp.concatenate([template, template_var], axis=0)
    patch_rows = owned_patch.shape[1]

    def cut_piece(column_start):
        return lax.dynamic_slice_in_dim(owned_patch, column_start, PIECE, 2)

    outgoing = jax.vmap(cut_piece)(starts.reshape(-1)) * filled.reshape(-1)[:, None, None, None]
    outgoing = outgoing.reshape(visits, slots, 2, patch_rows, PIECE)
    sources = lax.dynamic_index_in_dim(owner_of, owner_me, 0, keepdims=False)
    same_source = sources[:, None] == sources[None, :]
    earlier = jnp.arange(KP)[None, :] < jnp.arange(KP)[:, None]
    arrival = jnp.sum((same_source & earlier).astype(jnp.int32), axis=1)
    slot_index = sources * slots + arrival
    received = lax.all_to_all(outgoing, "visit", split_axis=0, concat_axis=0, tiled=True)
    item_rows = received.shape[3]
    stacked = received.reshape(visits * slots, 2, item_rows, PIECE)
    chosen = jnp.take(stacked, slot_index, axis=0)
    result = chosen.transpose(1, 2, 0, 3).reshape(2, item_rows, tile_width)
    operand = result[0:1]
    variance_rows = result[1]
    operand = with_halo(operand, (("tile", 1),), margin)
    row_pass = jnp.dot(
        row_band.reshape(tile_rows * NB, tile_rows + 2 * margin), operand[0], precision=highest
    )
    windows = column_windows(row_pass.reshape(tile_rows, NB, tile_width), margin)
    convolved = jnp.einsum("ibkw,bwc->ikc", windows, col_band, precision=highest).reshape(
        tile_rows, tile_width
    )
    difference = science - convolved[None]
    difference_var = science_var + kernel_power * variance_rows[None]
    return (difference, difference_var)


def solution(mesh):
    return jax.shard_map(
        local,
        mesh=mesh,
        in_specs=(
            P("visit", "tile", None),
            P("visit", "tile", None),
            P("visit", "tile", None),
            P("visit", "tile", None),
            P(),
            P(),
            P(),
            P(),
            P(),
            P(),
        ),
        out_specs=(P("visit", "tile", None), P("visit", "tile", None)),
        check_vma=False,
    )
```

profile of v0, /device:TPU:1, one launch (start us, length us, event | category | flops | bytes accessed | tf_op | source)
XLA Modules:
  0.0 436.0 jit_solution(16736645810453333534)
XLA Ops:
  0.7 0.8 broadcast_compare_fusion
  1.8 0.8 select_reduce_fusion
  2.8 4.9 %copy.37 = f32[1,64,4096]{1,0,2:T(1,128)S(1)} copy(f32[1,64,4096]{2,1,0:T(8,128)} %param.12) | data formatting | bytes 2097152 | tf_op args[2]
  7.7 5.3 %copy.38 = f32[1,64,4096]{1,0,2:T(1,128)} copy(f32[1,64,4096]{2,1,0:T(8,128)} %param.13) | data formatting | bytes 2097152 | tf_op args[3]
  13.0 7.4 %pad_maximum_fusion = f32[2,64,4096]{1,0,2:T(2,128)} fusion(f32[1,64,4096]{1,0,2:T(1,128)} %copy.38, f32[1,64,4096]{1,0,2:T(1,128)S(1)} %copy.37), kind=kLoop, calls=%fused_computation.4 | loop fusion | flops 524288 | bytes 4194304 | tf_op jit(solution)/shard_map/concatenate | solution.py:80
  20.4 13.6 %gather_fusion = f32[64,2,64,128]{2,1,3,0:T(2,128)} fusion(f32[2,64,4096]{1,0,2:T(2,128)} %pad_maximum_fusion, s32[64]{0:T(128)S(1)} %fusion.59), kind=kCustom, calls=%fused_computation | custom fusion | bytes 8389376 | tf_op jit(solution)/shard_map/vmap()/gather | solution.py:84
  34.0 11.4 %copy.41 = f32[32,2,2,64,128]{4,3,2,1,0:T(8,128)} copy(f32[32,2,2,64,128]{3,2,4,1,0:T(2,128)} %bitcast.185) | data formatting | bytes 8388608 | tf_op jit(solution)/shard_map/vmap()/gather | solution.py:84
  45.5 4.5 %broadcast_multiply_fusion = f32[32,2,2,64,128]{4,3,2,1,0:T(8,128)} fusion(f32[32,2,2,64,128]{4,3,2,1,0:T(8,128)} %copy.41, f32[32,2]{1,0:T(8,128)S(1)} %copy.40), kind=kLoop, calls=%fused_computation.8 | loop fusion | flops 1048576 | bytes 8388864 | tf_op jit(solution)/shard_map/mul | solution.py:86
  50.0 12.5 %all-to-all-start = ((f32[32,2,2,64,128]{4,3,2,1,0:T(8,128)}), f32[32,2,2,64,128]{4,3,2,1,0:T(8,128)}, u32[]{:S(2)}, u32[]{:S(2)}) async-start(f32[32,2,2,64,128]{4,3,2,1,0:T(8,128)} %broadcast_multiply_fusion), calls=%async_computation | async-start | bytes 8388608 | tf_op jit(solution)/shard_map/all_to_all | solution.py:93
  62.5 1.3 dynamic_slice.7
  63.8 0.7 fusion.63
  64.6 0.7 fusion.60
  65.3 0.8 convolution_bitcast_fusion.1
  66.1 0.9 fusion.45
  67.0 1.5 fusion.8
  68.6 0.7 compare_and_fusion
  69.2 1.4 fusion.9
  70.6 84.6 %all-to-all-done = f32[32,2,2,64,128]{4,3,2,1,0:T(8,128)} async-done(((f32[32,2,2,64,128]{4,3,2,1,0:T(8,128)}), f32[32,2,2,64,128]{4,3,2,1,0:T(8,128)}, u32[]{:S(2)}, u32[]{:S(2)}) %all-to-all-start) | async-done | bytes 4194336 | tf_op jit(solution)/shard_map/all_to_all | solution.py:93
  155.3 2.9 gather_fusion.1
  158.1 0.2 select_bitcast_fusion
  158.3 0.9 slice_multiply_fusion
  159.4 8.4 %collective-permute-start = (f32[1,20,4096]{2,1,0:T(8,128)S(1)}, f32[1,20,4096]{2,1,0:T(8,128)S(1)}, u32[]{:S(2)}, u32[]{:S(2)}) collective-permute-start(f32[1,20,4096]{2,1,0:T(8,128)S(1)} %get-tuple-element.12), channel_id=1, source_target_pairs={{0,1},{1,2},{2,3},{3,4},{4,5},{5,6},{6,7},{8,9},{9,10},{10,11},{11... | collective-permute-start | bytes 983048 | tf_op jit(solution)/shard_map/ppermute | solution.py:21
  167.8 2.1 collective-permute-start.1
  169.9 0.6 copy.44
  170.5 2.8 copy_add_fusion
  173.3 1.6 copy.46
  174.9 2.0 collective-permute-done.1
  176.9 14.7 %fusion.2 = f32[64,16,4096]{2,1,0:T(8,128)S(1)} fusion(f32[64,16,104]{2,1,0:T(8,128)} %fusion.9, f32[1,20,4096]{2,1,0:T(8,128)S(1)} %collective-permute-done.1, f32[1,64,4096]{2,1,0:T(8,128)S(1)} %bitcast.187, f32[1,20,4096]{2,1,0:T(8,128)S(1)} %collective-permute-done), kind=kOutput, calls=%fused_computation.11 | convolution fusion | flops 5235343360 | bytes 18907136 | tf_op jit(solution)/shard_map/dot_general | solution.py:101
  191.6 1.3 fusion.11
  192.9 1.4 fusion.43
  194.3 1.3 fusion.42
  195.6 1.3 fusion.41
  196.9 1.4 fusion.40
  198.3 1.3 fusion.39
  199.6 1.3 fusion.38
  200.9 1.3 fusion.37
  202.3 1.4 fusion.36
  203.7 1.3 fusion.35
  205.0 1.3 fusion.34
  206.3 1.3 fusion.33
  207.6 1.3 fusion.32
  208.9 1.3 fusion.31
  210.2 1.3 fusion.30
  211.5 1.3 fusion.29
  212.8 1.3 fusion.28
  214.2 1.3 fusion.27
  215.5 1.3 fusion.26
  216.8 1.4 fusion.25
  218.2 1.3 fusion.24
  219.5 1.4 fusion.23
  220.9 1.3 fusion.22
  222.2 1.3 fusion.21
  223.5 1.3 fusion.20
  224.8 1.4 fusion.19
  226.2 1.5 fusion.18
  227.7 1.3 fusion.17
  229.0 1.3 fusion.16
  230.3 1.3 fusion.15
  231.6 1.3 fusion.14
  232.9 1.3 fusion.13
  234.3 55.8 %copy.43 = f32[64,16,32,168]{2,1,3,0:T(8,128)} copy(f32[64,16,32,168]{3,1,0,2:T(8,128)} %fusion.13) | data formatting | bytes 44040192 | tf_op jit(solution)/shard_map/stack | solution.py:32
  290.1 143.1 %convolution_bitcast_fusion = f32[64,32,128]{2,1,0:T(8,128)S(1)} fusion(f32[64,16,32,168]{2,1,3,0:T(8,128)} %copy.43, f32[16,168,128,1]{2,0,1,3:T(8,128)S(1)} %fusion.8), kind=kOutput, calls=%fused_computation.19 | convolution fusion | flops 8455716864 | bytes 24444928 | tf_op jit(solution)/shard_map/ibkw,bwc->ikc/dot_general | solution.py:105
  433.2 0.2 broadcast_in_dim_reshape.4
  433.4 2.4 sub.48
  (24 shorter events, 1.0 us)
Async XLA Ops:
  0.6 65.4 %copy-start = (f32[16,41]{1,0:T(8,128)S(1)}, f32[16,41]{1,0:T(8,128)}, u32[]{:S(2)}) copy-start(f32[16,41]{1,0:T(8,128)} %param.17) | copy-start | bytes 7876
  0.6 64.6 %copy-start.3 = (f32[8,16]{1,0:T(8,128)S(1)}, f32[8,16]{1,0:T(8,128)}, u32[]{:S(2)}) copy-start(f32[8,16]{1,0:T(8,128)} %param.18) | copy-start | bytes 1540
  0.7 65.4 %copy-start.2 = (f32[16,41]{1,0:T(8,128)S(1)}, f32[16,41]{1,0:T(8,128)}, u32[]{:S(2)}) copy-start(f32[16,41]{1,0:T(8,128)} %param.16) | copy-start | bytes 7876
  50.0 105.3 %all-to-all-start = ((f32[32,2,2,64,128]{4,3,2,1,0:T(8,128)}), f32[32,2,2,64,128]{4,3,2,1,0:T(8,128)}, u32[]{:S(2)}, u32[]{:S(2)}) async-start(f32[32,2,2,64,128]{4,3,2,1,0:T(8,128)} %broadcast_multiply_fusion), calls=%async_computation | async-start | bytes 8388608 | tf_op jit(solution)/shard_map/all_to_all | solution.py:93
  159.4 15.5 %collective-permute-start = (f32[1,20,4096]{2,1,0:T(8,128)S(1)}, f32[1,20,4096]{2,1,0:T(8,128)S(1)}, u32[]{:S(2)}, u32[]{:S(2)}) collective-permute-start(f32[1,20,4096]{2,1,0:T(8,128)S(1)} %get-tuple-element.12), channel_id=1, source_target_pairs={{0,1},{1,2},{2,3},{3,4},{4,5},{5,6},{6,7},{8,9},{9,10},{10,11},{11... | collective-permute-start | bytes 983048 | tf_op jit(solution)/shard_map/ppermute | solution.py:21
  167.8 9.1 %collective-permute-start.1 = (f32[1,20,4096]{2,1,0:T(8,128)S(1)}, f32[1,20,4096]{2,1,0:T(8,128)S(1)}, u32[]{:S(2)}, u32[]{:S(2)}) collective-permute-start(f32[1,20,4096]{2,1,0:T(8,128)S(1)} %get-tuple-element.13), channel_id=1, source_target_pairs={{1,0},{2,1},{3,2},{4,3},{5,4},{6,5},{7,6},{9,8},{10,9},{11,10},{12... | collective-permute-start | bytes 983048 | tf_op jit(solution)/shard_map/ppermute | solution.py:23
  234.3 201.5 %copy-start.1 = (f32[16,41]{1,0:T(8,128)S(1)}, f32[16,41]{1,0:T(8,128)}, u32[]{:S(2)}) copy-start(f32[16,41]{1,0:T(8,128)} %param.17) | copy-start | bytes 7876
where the time goes:
time: 445 us; the launch traced here: 436 us
  matrix products  162 us (36%)
  local copies, waits for them, and re-layouts  141 us (32%)
  waiting for transfers between devices  86.6 us (19%)
  starting transfers between devices  23 us (5%)
  other arithmetic  21.6 us (5%)
    dot_general x1, matrix products, local(): jnp.einsum('ibkw,bwc->ikc', windows, col_band, precision=highest)  143 us
    all_to_all x1, waiting for transfers between devices, local(): lax.all_to_all(outgoing, 'visit', split_axis=0, concat_axis=0, tiled=True)  84.6 us
    another operation x2, local copies, waits for them, and re-layouts, column_windows(): jnp.stack([padded[..., column_block * PIECE:column_block * PIECE + PIECE...  57.1 us
    unnamed x42, local copies, waits for them, and re-layouts  53.2 us
    gather x2, local copies, waits for them, and re-layouts, cut_piece(): return lax.dynamic_slice_in_dim(owned_patch, column_start, PIECE, 2)  25 us
    dot_general x1, matrix products, local(): jnp.dot(row_band.reshape(tile_rows * NB, tile_rows + 2 * margin), operand...  14.7 us
    all_to_all x1, starting transfers between devices, local(): lax.all_to_all(outgoing, 'visit', split_axis=0, concat_axis=0, tiled=True)  12.5 us
  transfers between devices with their start and end apart: 3, of which 2 were waited for; matrix products, arithmetic and copies ran while one was open for 3% of the time, Pallas kernels for 0%

commit v1 on v0

v1 whole, which is shorter than its diff:
```python
import functools

import jax
import jax.numpy as jnp
from jax import lax
from jax.experimental import pallas as pl
from jax.experimental.pallas import tpu as pltpu
from jax.sharding import PartitionSpec as P

MESH = pl.DeviceIdType.MESH
F32 = jnp.float32
BF16 = jnp.bfloat16

TR = 64
PIECE = 128
KP = 32
KW = 41
MARGIN = 20
NB = 16
NSETS = 8
TILES = 8
WIDTH = 4096
NY = 4
NZ = 8
CAP = 2
PER_ROW = NZ * CAP
CHUNK = 16
PARTS = TR // CHUNK
NC = 2 * PARTS
HALO = 24
XROWS = 128
WIN = 384
OUTW = 256
NWIN = WIDTH // OUTW
XBLOCKS = 34
GROUP = 4
NGROUPS = NB // GROUP


def pack_kernel(starts, flux, var, out):
    row = lax.rem(lax.axis_index("visit") // NZ + pl.program_id(0), NY)
    lane = lax.broadcasted_iota(jnp.int32, (TR, PIECE), 1)

    def one(slot, _):
        start = starts[row * PER_ROW + slot]
        block = start // PIECE
        shift = lax.rem(start, PIECE)
        low = pl.multiple_of(block * PIECE, PIECE)
        high = pl.multiple_of(jnp.minimum(block + 1, KP - 1) * PIECE, PIECE)
        turn = PIECE - shift
        for plane, ref in enumerate((flux, var)):
            piece = jnp.where(
                lane < turn,
                pltpu.roll(ref[:, pl.ds(low, PIECE)], turn, 1),
                pltpu.roll(ref[:, pl.ds(high, PIECE)], turn, 1),
            )
            for part in range(PARTS):
                out[plane * PARTS + part, 0, slot] = piece[part * CHUNK : (part + 1) * CHUNK]
        return 0

    lax.fori_loop(0, PER_ROW, one, 0)


def pack(starts, flux, var):
    return pl.pallas_call(
        pack_kernel,
        grid_spec=pltpu.PrefetchScalarGridSpec(
            num_scalar_prefetch=1,
            grid=(NY,),
            in_specs=[pl.BlockSpec((TR, WIDTH), lambda r, s: (0, 0))] * 2,
            out_specs=pl.BlockSpec((NC, 1, PER_ROW, CHUNK, PIECE), lambda r, s: (0, r, 0, 0, 0)),
        ),
        out_shape=jax.ShapeDtypeStruct((NC, NY, PER_ROW, CHUNK, PIECE), F32),
        compiler_params=pltpu.CompilerParams(vmem_limit_bytes=32 << 20),
        name="pack",
    )(starts, flux, var)


def split(x):
    high = x.astype(BF16)
    return high, (x - high.astype(F32)).astype(BF16)


def main_kernel(slots, *refs):
    (shift_of, place_of, pick_of, tile_coef, coefs, packed, brow, bcol) = refs[:8]
    conv, var_out, power = refs[8:11]
    yr, zs, zr = refs[11 : 11 + NC], refs[11 + NC : 11 + 2 * NC], refs[11 + 2 * NC : 11 + 3 * NC]
    (x_full, x_split, row_band, cb_high, cb_low, rw_high, rw_low, acc) = refs[11 + 3 * NC : 19 + 3 * NC]
    (own_sem, ys_sem, yr_sem, zs_sem, zr_sem, hs_sem, hr_sem) = refs[19 + 3 * NC :]

    me = lax.axis_index("visit")
    tile = lax.axis_index("tile")
    y, z = me // NZ, lax.rem(me, NZ)

    def y_peer(r):
        return (lax.rem(y + r, NY) * NZ + z, tile)

    def z_peer(d):
        return (y * NZ + lax.rem(z + d, NZ), tile)

    def t_peer(s):
        return (me, lax.rem(tile + s + TILES, TILES))

    barrier = pltpu.get_barrier_semaphore()
    peers = [y_peer(r) for r in range(1, NY)] + [z_peer(d) for d in range(1, NZ)] + [t_peer(1), t_peer(-1)]
    for peer in peers:
        pl.semaphore_signal(barrier, inc=1, device_id=peer, device_id_type=MESH)
    pl.semaphore_wait(barrier, len(peers))

    def y_copy(c, r):
        return pltpu.make_async_remote_copy(
            src_ref=packed.at[c, r],
            dst_ref=yr[c].at[pl.ds(r * PER_ROW, PER_ROW)],
            send_sem=ys_sem.at[c, r - 1],
            recv_sem=yr_sem.at[c, r - 1],
            device_id=y_peer(r),
            device_id_type=MESH,
        )

    def own_copy(c):
        return pltpu.make_async_copy(packed.at[c, 0], yr[c].at[pl.ds(0, PER_ROW)], own_sem.at[c])

    def z_copy(c, d):
        return pltpu.make_async_remote_copy(
            src_ref=zs[c].at[pl.ds(d * slots, slots)],
            dst_ref=zr[c].at[pl.ds(d * slots, slots)],
            send_sem=zs_sem.at[c, d - 1],
            recv_sem=zr_sem.at[c, d - 1],
            device_id=z_peer(d),
            device_id_type=MESH,
        )

    def halo_copy(which):
        source, target, step = ((TR, 0, 1), (HALO, HALO + TR, -1))[which]
        return pltpu.make_async_remote_copy(
            src_ref=x_full.at[pl.ds(source, HALO)],
            dst_ref=x_full.at[pl.ds(target, HALO)],
            send_sem=hs_sem.at[which],
            recv_sem=hr_sem.at[which],
            device_id=t_peer(step),
            device_id_type=MESH,
        )

    def y_start(c):
        for r in (2, 1, 3):
            y_copy(c, r).start()
        own_copy(c).start()

    def forward(c):
        own_copy(c).wait()
        for r in range(1, NY):
            y_copy(c, r).wait_recv()

        def one(e, _):
            half = (e + 1) // 2
            d = NZ // 2 + jnp.where(lax.rem(e, 2) == 1, -half, half)
            base = (y * NZ + lax.rem(z + d, NZ)) * NZ
            for p in range(slots):
                zs[c][d * slots + p] = yr[c][pick_of[base + p]]
            z_copy(c, d).start()
            return 0

        lax.fori_loop(0, NZ - 1, one, 0)
        for p in range(slots):
            zr[c][p] = yr[c][pick_of[me * NZ + p]]

    def assemble(c, out, row):
        for d in range(1, NZ):
            z_copy(c, d).wait_recv()

        def one(k, _):
            at = shift_of[me * KP + k] * slots + place_of[me * KP + k]
            out[pl.ds(row, CHUNK), pl.ds(pl.multiple_of(k * PIECE, PIECE), PIECE)] = zr[c][at]
            return 0

        lax.fori_loop(0, KP, one, 0)

    chosen = tile_coef[me * TILES + tile]

    def bands():
        rows = [coefs[chosen * NB + b] * brow[b : b + 1, :] for b in range(NB)]
        for b in range(NB):
            band = pltpu.roll(jnp.broadcast_to(rows[b], (TR, PIECE)), 0, 1, stride=1, stride_axis=0)
            high, low = split(band)
            row_band[b * TR : (b + 1) * TR, 0:PIECE] = high
            row_band[b * TR : (b + 1) * TR, PIECE : 2 * PIECE] = low
            row_band[b * TR : (b + 1) * TR, 2 * PIECE : 3 * PIECE] = high
        whole = lax.dot_general(
            jnp.concatenate(rows, axis=0),
            bcol[...],
            (((0,), (0,)), ((), ())),
            precision=lax.Precision.HIGHEST,
            preferred_element_type=F32,
        )
        power[...] = jnp.full((8, PIECE), jnp.sum(whole * whole), F32)

        def one(b, _):
            line = bcol[pl.ds(b, 1), :]
            for part in range(WIN // 128):
                turned = pltpu.roll(
                    jnp.broadcast_to(line, (128, OUTW)), (part * 128) % OUTW, 1, stride=1, stride_axis=0
                )
                tap = (
                    lax.broadcasted_iota(jnp.int32, (128, OUTW), 0)
                    + part * 128
                    - lax.broadcasted_iota(jnp.int32, (128, OUTW), 1)
                )
                high, low = split(jnp.where((tap >= 0) & (tap < KW), turned, 0.0))
                place = pl.ds(pl.multiple_of(b * WIN + part * 128, 128), 128)
                cb_high[place, :] = high
                cb_low[place, :] = low
            return 0

        lax.fori_loop(0, NB, one, 0)

    def expand():
        row = lax.broadcasted_iota(jnp.int32, (XROWS, PIECE), 0)
        lane = lax.broadcasted_iota(jnp.int32, (XROWS, PIECE), 1)
        first = jnp.where(tile == 0, HALO, 0)
        last = jnp.where(tile == TILES - 1, HALO + TR, HALO + TR + HALO)
        rows_in = (row >= first) & (row < last)

        def one(j, _):
            here = pl.multiple_of(jnp.minimum(j, KP - 1) * PIECE, PIECE)
            before = pl.multiple_of(jnp.minimum(jnp.maximum(j - 1, 0), KP - 1) * PIECE, PIECE)
            both = jnp.where(
                lane < MARGIN,
                pltpu.roll(x_full[:, pl.ds(before, PIECE)], MARGIN, 1),
                pltpu.roll(x_full[:, pl.ds(here, PIECE)], MARGIN, 1),
            )
            column = j * PIECE + lane - MARGIN
            high, low = split(jnp.where(rows_in & (column >= 0) & (column < WIDTH), both, 0.0))
            place = pl.ds(pl.multiple_of(j * PIECE, PIECE), PIECE)
            x_split[0:XROWS, place] = high
            x_split[XROWS : 2 * XROWS, place] = high
            x_split[2 * XROWS : 3 * XROWS, place] = low
            return 0

        lax.fori_loop(0, XBLOCKS, one, 0)

    def convolve(g):
        def rows(m, _):
            high, low = split(
                jnp.dot(
                    row_band[g * GROUP * TR : (g + 1) * GROUP * TR, :],
                    x_split[:, pl.ds(pl.multiple_of(m * OUTW, OUTW), OUTW)],
                    preferred_element_type=F32,
                )
            )
            now = pl.ds(pl.multiple_of((m + 1) * TR, TR), TR)
            earlier = pl.ds(pl.multiple_of(m * TR, TR), TR)
            for out, value in ((rw_high, high), (rw_low, low)):
                for b in range(GROUP):
                    part = value[b * TR : (b + 1) * TR]
                    out[now, b * WIN : b * WIN + OUTW] = part
                    out[earlier, b * WIN + OUTW : (b + 1) * WIN] = part[:, 0 : WIN - OUTW]
            return 0

        lax.fori_loop(0, NWIN + 1, rows, 0)
        band = slice(g * GROUP * WIN, (g + 1) * GROUP * WIN)

        def cols(m, _):
            at = pl.ds(pl.multiple_of(TR + m * 512, TR), 512)
            high = rw_high[at, :]
            total = jnp.dot(high, cb_high[band, :], preferred_element_type=F32)
            total += jnp.dot(high, cb_low[band, :], preferred_element_type=F32)
            total += jnp.dot(rw_low[at, :], cb_high[band, :], preferred_element_type=F32)
            place = pl.ds(pl.multiple_of(m * 512, 512), 512)
            acc[place, :] = total if g == 0 else acc[place, :] + total
            return 0

        lax.fori_loop(0, NWIN * TR // 512, cols, 0)

    y_start(0)
    y_start(1)
    y_start(2)
    for c in range(NC):
        forward(c)
        if c + 3 < NC:
            y_start(c + 3)
        if c == PARTS - 1:
            bands()
        if c == NC - 3:
            for part in range(PARTS):
                assemble(part, x_full, HALO + part * CHUNK)
            halo_copy(0).start()
            halo_copy(1).start()
        if c == NC - 2:
            halo_copy(0).wait_recv()
            halo_copy(1).wait_recv()
            expand()
            convolve(0)
    for g in range(1, NGROUPS):
        convolve(g)
    for n in range(NWIN):
        conv[:, n * OUTW : (n + 1) * OUTW] = acc[n * TR : (n + 1) * TR, :]
    for part in range(PARTS):
        assemble(PARTS + part, var_out, part * CHUNK)
    halo_copy(0).wait_send()
    halo_copy(1).wait_send()
    for c in range(NC):
        for r in range(1, NY):
            y_copy(c, r).wait_send()
        for d in range(1, NZ):
            z_copy(c, d).wait_send()


def exchange(slots, shift_of, place_of, pick_of, tile_coef, coefs, packed, brow, bcol):
    smem = pl.BlockSpec(memory_space=pltpu.SMEM)
    vmem = pl.BlockSpec(memory_space=pltpu.VMEM)
    scratch = [pltpu.VMEM((NY * PER_ROW, CHUNK, PIECE), F32)] * NC
    scratch += [pltpu.VMEM((NZ * slots, CHUNK, PIECE), F32)] * (2 * NC)
    scratch += [
        pltpu.VMEM((XROWS, WIDTH), F32),
        pltpu.VMEM((3 * XROWS, XBLOCKS * PIECE), BF16),
        pltpu.VMEM((NB * TR, 3 * PIECE), BF16),
        pltpu.VMEM((NB * WIN, OUTW), BF16),
        pltpu.VMEM((NB * WIN, OUTW), BF16),
        pltpu.VMEM(((NWIN + 2) * TR, GROUP * WIN), BF16),
        pltpu.VMEM(((NWIN + 2) * TR, GROUP * WIN), BF16),
        pltpu.VMEM((NWIN * TR, OUTW), F32),
        pltpu.SemaphoreType.DMA((NC,)),
        pltpu.SemaphoreType.DMA((NC, NY - 1)),
        pltpu.SemaphoreType.DMA((NC, NY - 1)),
        pltpu.SemaphoreType.DMA((NC, NZ - 1)),
        pltpu.SemaphoreType.DMA((NC, NZ - 1)),
        pltpu.SemaphoreType.DMA((2,)),
        pltpu.SemaphoreType.DMA((2,)),
    ]
    return pl.pallas_call(
        functools.partial(main_kernel, slots),
        out_shape=(
            jax.ShapeDtypeStruct((TR, WIDTH), F32),
            jax.ShapeDtypeStruct((TR, WIDTH), F32),
            jax.ShapeDtypeStruct((8, PIECE), F32),
        ),
        in_specs=[smem] * 5 + [pl.BlockSpec(memory_space=pl.ANY)] + [vmem] * 2,
        out_specs=(vmem, vmem, vmem),
        scratch_shapes=scratch,
        compiler_params=pltpu.CompilerParams(
            collective_id=slots, has_side_effects=True, vmem_limit_bytes=56 << 20
        ),
        cost_estimate=pl.CostEstimate(flops=10**10, bytes_accessed=6 << 20, transcendentals=0),
        name=f"exchange_{slots}",
    )(shift_of, place_of, pick_of, tile_coef, coefs, packed, brow, bcol)


VARIANTS = (5, 6, 8)


def local(
    science,
    science_var,
    template,
    template_var,
    intersection,
    col_offset,
    basis_row,
    basis_col,
    coef_sets,
    tile_coef,
):
    me = lax.axis_index("visit")
    my_y, my_z = me // NZ, me % NZ
    owner = intersection[:, :, 0]
    column = owner % NZ
    earlier = jnp.arange(KP)[None, None, :] < jnp.arange(KP)[None, :, None]
    rank = jnp.sum(((owner[:, :, None] == owner[:, None, :]) & earlier).astype(jnp.int32), axis=2)
    place = jnp.sum(((column[:, :, None] == column[:, None, :]) & earlier).astype(jnp.int32), axis=2)
    mine = (owner == me)[:, None, :] & (rank[:, None, :] == jnp.arange(CAP)[None, :, None])
    starts = jnp.sum(jnp.where(mine, col_offset[:, None, :], 0), axis=2).reshape(-1)
    came_from = (my_y - owner // NZ) % NY
    visit_z = jnp.arange(KP, dtype=jnp.int32)[:, None] % NZ
    slot = came_from * PER_ROW + visit_z * CAP + rank
    here = (column == my_z)[:, None, :] & (place[:, None, :] == jnp.arange(NZ)[None, :, None])
    pick = jnp.sum(jnp.where(here, slot[:, None, :], 0), axis=2).reshape(-1)
    shift = ((visit_z - column) % NZ).reshape(-1)
    most = jnp.max(place) + 1

    packed = pack(starts, template[0], template_var[0])
    brow = jnp.pad(basis_row, ((0, 0), (HALO - MARGIN, PIECE - KW - HALO + MARGIN)))
    bcol = jnp.concatenate(
        [basis_col[:, 0:1], jnp.zeros((NB, OUTW - KW), F32), basis_col[:, :0:-1]], axis=1
    )
    which = sum((most > n).astype(jnp.int32) for n in VARIANTS[:-1])
    convolved, variance, power = lax.switch(
        which,
        [functools.partial(exchange, n) for n in VARIANTS],
        shift,
        place.reshape(-1),
        pick,
        tile_coef.reshape(-1),
        coef_sets.reshape(-1),
        packed,
        brow,
        bcol,
    )
    difference = science - convolved[None]
    difference_var = science_var + power[0, 0] * variance[None]
    return difference, difference_var


def solution(mesh):
    split3 = P("visit", "tile", None)
    return jax.shard_map(
        local,
        mesh=mesh,
        in_specs=(split3, split3, split3, split3, P(), P(), P(), P(), P(), P()),
        out_specs=(split3, split3),
        check_vma=False,
    )
```

time: 445 us -> 125 us (0.28); the launches traced: 436 us -> 124 us
  matrix products: 162 us -> 0 us
  local copies, waits for them, and re-layouts: 141 us -> 8.31 us
  Pallas kernels: 0 us -> 101 us
  waiting for transfers between devices: 86.6 us -> 0 us
  starting transfers between devices: 23 us -> 0 us
  other arithmetic: 21.6 us -> 12.5 us
    dot_general x6 -> x0, matrix products: 162 us -> none  [the longest x1 143 us: local(): jnp.einsum('ibkw,bwc->ikc', windows, col_band, precision=highest)]
    pallas_call x0 -> x2, Pallas kernels: none -> 101 us  [the longest x1 92.4 us: exchange(): pl.pallas_call(functools.partial(main_kernel, slots), out_shape=(jax.Shap...]
    all_to_all x1 -> x0, waiting for transfers between devices: 84.6 us -> none  [local(): lax.all_to_all(outgoing, 'visit', split_axis=0, concat_axis=0, tiled=True)]
    another operation x3 -> x4, local copies, waits for them, and re-layouts: 57.3 us -> 0.08 us  [the longest x2 57.1 us: column_windows(): jnp.stack([padded[..., column_block * PIECE:column_block * PIECE + PIECE...]
    unnamed x42 -> x15, local copies, waits for them, and re-layouts: 53.2 us -> 2.98 us
    gather x3 -> x0, local copies, waits for them, and re-layouts: 27.9 us -> none  [the longest x2 25 us: cut_piece(): return lax.dynamic_slice_in_dim(owned_patch, column_start, PIECE, 2)]
    all_to_all x1 -> x0, starting transfers between devices: 12.5 us -> none  [local(): lax.all_to_all(outgoing, 'visit', split_axis=0, concat_axis=0, tiled=True)]
    ppermute x2 -> x0, starting transfers between devices: 10.5 us -> none  [the longest x1 8.38 us: with_halo(): lax.ppermute(tail, axis, [(i, (i + 1) % count) for i in range(ends)])]
  transfers between devices with their start and end apart: 3 -> 0, of which waited for: 2 -> 0; matrix products, arithmetic and copies ran while one was open for 3% -> 0% of each run, Pallas kernels for 0% -> 0%
where the time goes in v1:
time: 125 us; the launch traced here: 124 us
  Pallas kernels  101 us (81%)
  other arithmetic  12.5 us (10%)
  local copies, waits for them, and re-layouts  8.31 us (7%)
  between operations  1.45 us (1%)
    pallas_call x1, Pallas kernels, exchange(): pl.pallas_call(functools.partial(main_kernel, slots), out_shape=(jax.Shap...  92.4 us
    pallas_call x1, Pallas kernels, pack(): pl.pallas_call(pack_kernel, grid_spec=pltpu.PrefetchScalarGridSpec(num_sc...  8.68 us
    unnamed x15, local copies, waits for them, and re-layouts  2.98 us

profile of v1, /device:TPU:1, one launch (start us, length us, event | category | flops | bytes accessed | tf_op | source)
XLA Modules:
  0.0 123.7 jit_solution(14464786242544573072)
XLA Ops:
  0.6 0.0 copy-start.5
  0.6 0.0 copy-start.6
  0.7 0.0 copy-start.4
  0.7 0.1 pad.18.clone
  0.8 0.7 broadcast_compare_fusion
  1.5 0.8 slice.10
  2.3 0.1 rev.3
  2.4 0.8 pad_maximum_fusion
  3.1 0.7 broadcast_compare_fusion.2
  3.9 0.1 sub.37
  3.9 0.1 sub.38
  4.0 0.7 add_select_fusion.10
  4.8 0.7 fusion.24
  5.5 0.5 broadcast.288
  6.0 1.5 %fusion.30 = (s32[32,32]{1,0:T(8,128)S(1)}, s32[32,32,1]{1,2,0:T(1,128)S(1)}) fusion(s32[32,32,1]{1,2,0:T(1,128)} %param.17, s32[]{:T(128)} %broadcast.288), kind=kLoop, calls=%fused_computation.87 | loop fusion | flops 11264 | bytes 12292 | tf_op args[4]
  7.5 0.1 squeeze.17
  7.5 2.2 %convert_reduce_fusion = (s32[32,32]{1,0:T(8,128)S(1)}, s32[32,32]{1,0:T(8,128)S(1)}) fusion(s32[32,32]{1,0:T(8,128)} %bitcast.42, pred[32,32]{1,0:T(8,128)(4,1)S(1)} %iota_compare_fusion.1, s32[32,32]{1,0:T(8,128)S(1)} %add_select_fusion.10, s32[32,32]{1,0:T(8,128)S(1)} %bitcast.43), kind=kLoop, calls=%fused_computation.50 | loop fusion | flops 260096 | bytes 21504 | tf_op jit(solution)/shard_map/reduce_sum | solution.py:368
  9.8 0.6 reduce_max.9
  11.1 0.8 select_reduce_fusion.3
  11.9 0.1 copy.33
  12.0 0.1 reshape.263.starts
  12.2 0.0 copy-start
  12.2 1.2 copy-done
  13.4 0.0 copy-start.1
  13.4 1.2 copy-done.1
  14.6 8.7 %pack.1 = f32[8,4,16,16,128]{4,3,2,1,0:T(8,128)} custom-call(s32[64]{0:T(128)S(1)} %reshape.263.starts, f32[64,4096]{1,0:T(8,128)S(1)} %bitcast.36, f32[64,4096]{1,0:T(8,128)S(1)} %bitcast.37), custom_call_target="tpu_custom_call" | custom-call | tf_op jit(solution)/shard_map/pack/pallas_call | solution.py:65
  23.3 0.0 copy-done.5
  23.3 0.0 copy-done.6
  23.3 0.0 copy-done.4
  23.3 0.0 copy-start.2
  23.3 0.0 copy-start.3
  23.4 97.5 %conditional.1 = ((f32[64,4096]{1,0:T(8,128)S(1)}, f32[64,4096]{1,0:T(8,128)S(1)}, f32[8,128]{1,0:T(8,128)S(1)})) conditional(s32[]{:T(128)} %clamp.3, (pred[1024]{0:T(1024)(128)(4,1)S(1)}, s32[1024]{0:T(1024)S(1)}, s32[1024]{0:T(1024)S(1)}, s32[32,32]{1,0:T(8,128)S(1)}, s32[]{:T(128)}, ...), branch_computations={%region_4.6_spmd.clone, %region_6.8_spmd.clone, %region_8.10_spmd.... | conditional | flops 10000055296 | bytes 6423046 | solution.py:386
  23.4 0.1 fusion.3
  23.5 0.6 select_reduce_fusion
  24.1 0.6 reshape.265.refs_2_
  24.8 0.7 reshape.264.refs_1_
  25.4 0.7 reshape.267.refs_4_
  26.1 0.6 add_select_fusion.2.refs_0_
  26.7 0.7 pad.14.refs_6_
  27.3 0.1 copy.34
  27.4 0.7 reshape.266.refs_3_
  28.1 92.4 %exchange_5.2 = (f32[64,4096]{1,0:T(8,128)S(1)}, f32[64,4096]{1,0:T(8,128)S(1)}, f32[8,128]{1,0:T(8,128)S(1)}) custom-call(s32[1024]{0:T(1024)} %add_select_fusion.2.refs_0_, s32[1024]{0:T(1024)} %reshape.264.refs_1_, s32[256]{0:T(256)} %reshape.265.refs_2_, s32[256]{0:T(256)} %reshape.266.refs_3_, f32[128]{0:T(128)} %reshape.267.refs_4_, ...), custom_call_target="tpu_custom_call" | custom-call | flops 10000000000 | bytes 6291456 | tf_op jit(solution)/shard_map/cond/branch_0_fun/exchange_5/pallas_call | solution.py:330
  120.8 0.6 slice.11
  121.4 0.0 copy-done.2
  121.4 0.0 copy-done.3
  121.4 2.3 %bitcast_add_fusion = (f32[1,64,4096]{2,1,0:T(8,128)}, f32[1,64,4096]{2,1,0:T(8,128)}) fusion(f32[1,64,4096]{2,1,0:T(8,128)S(1)} %copy-done.2, f32[64,4096]{1,0:T(8,128)S(1)} %get-tuple-element.1052, f32[]{:T(128)} %bitcast.6, f32[1,64,4096]{2,1,0:T(8,128)S(1)} %copy-done.3, f32[64,4096]{1,0:T(8,128)S(1)} %get-tuple-element.1050), kind=kLoop, calls=%fused_computation.48 | loop fusion | flops 786432 | bytes 6291460 | tf_op jit(solution)/shard_map/add | solution.py:399
  (13 shorter events, 0.1 us)
Async XLA Ops:
  0.6 22.7 %copy-start.5 = (s32[32,8]{0,1:T(8,128)S(1)}, s32[32,8]{0,1:T(8,128)}, u32[]{:S(2)}) copy-start(s32[32,8]{0,1:T(8,128)} %param.22) | copy-start | bytes 3076
  0.6 22.7 %copy-start.6 = (f32[8,16]{1,0:T(8,128)S(1)}, f32[8,16]{1,0:T(8,128)}, u32[]{:S(2)}) copy-start(f32[8,16]{1,0:T(8,128)} %param.21) | copy-start | bytes 1540
  0.7 22.7 %copy-start.4 = (f32[16,41]{1,0:T(8,128)S(1)}, f32[16,41]{1,0:T(8,128)}, u32[]{:S(2)}) copy-start(f32[16,41]{1,0:T(8,128)} %param.19) | copy-start | bytes 7876
  12.2 1.2 copy-start
  13.4 1.2 copy-start.1
  23.3 98.1 %copy-start.2 = (f32[1,64,4096]{2,1,0:T(8,128)S(1)}, f32[1,64,4096]{2,1,0:T(8,128)}, u32[]{:S(2)}) copy-start(f32[1,64,4096]{2,1,0:T(8,128)} %param.14) | copy-start | bytes 3145732
  23.3 98.1 %copy-start.3 = (f32[1,64,4096]{2,1,0:T(8,128)S(1)}, f32[1,64,4096]{2,1,0:T(8,128)}, u32[]{:S(2)}) copy-start(f32[1,64,4096]{2,1,0:T(8,128)} %param.13) | copy-start | bytes 3145732
